TPU v7x, 128 devices: a whole 4x4x4 slice. The times are simulated.
128 devices in a mesh: gx: 4 (over y), gy: 4 (over x_hi, core), gz: 8 (over z, x_lo).
Axes of the slice: x: 4 (x_hi: 2, x_lo: 2; x = x_hi * 2 + x_lo), y: 4, z: 4, core: 2. Of those that a mesh axis runs over, the one named last changes fastest.
Arguments:
- initial_state: float32 [2, 4, 4, 8, 131072], P(None, 'gx', 'gy', 'gz'), may hold values from -6 to 6
- local_gates: float32 [3, 2, 128, 128], replicated, may hold values from -0.375 to 0.375
- top_gates: float32 [2, 2, 128, 128], replicated, may hold values from -1 to 1
- placement: int32 [5, 7], replicated, may hold values from 0 to 6, each once within a row
- damping: float32 [7], replicated, may hold values from 0.05 to 0.5
- branches: int32 [7], replicated, may hold values from 0 to 1
- outcomes: int32 [4], replicated, may hold values from 0 to 1, as said below
Outputs:
- collapsed: float32 [2, 4, 4, 8, 131072], P(None, 'gx', 'gy', 'gz')
- probability: float32 [], replicated
Inputs may be any that keep to these rules, and one draw needn't show every extreme that they name: `placement`: each row is a permutation of 0 to 6. `outcomes`: the four entries are not all equal.
All inputs are finite; a program needn't handle non-finite values.
Results may differ from a plain program's by a relative error of at most 0.0003.
Values sent between devices are 32-bit elements; how exact they have to be, the bound alone decides.
A program may use at most 64 MiB of HBM per device.

v0:
```python
import jax
import jax.numpy as jnp
from jax import lax
from jax.sharding import PartitionSpec as P


def oriented(gate, leg_order):
    lanes = jnp.arange(128, dtype=jnp.int32)
    source = jnp.zeros((128,), jnp.int32)
    for bit_pos in range(7):
        picked = jnp.bitwise_and(jnp.right_shift(lanes, leg_order[bit_pos]), 1)
        source = source + jnp.left_shift(picked, bit_pos)
    selector_matrix = (source[:, None] == lanes[None, :]).astype(jnp.float32)
    highest = lax.Precision.HIGHEST
    return tuple(
        (
            jnp.dot(
                jnp.dot(selector_matrix, gate[part_index], precision=highest),
                selector_matrix.T,
                precision=highest,
            )
            for part_index in range(2)
        )
    )


def kraus_matrix(damping, branches):
    lanes = jnp.arange(128, dtype=jnp.int32)
    result = jnp.ones((128, 128), jnp.float32)
    for bit_pos in range(7):
        row_bit = jnp.bitwise_and(jnp.right_shift(lanes, bit_pos), 1)[:, None]
        col_bit = jnp.bitwise_and(jnp.right_shift(lanes, bit_pos), 1)[None, :]
        staying = jnp.where(
            row_bit == col_bit, jnp.where(row_bit == 1, jnp.sqrt(1.0 - damping[bit_pos]), 1.0), 0.0
        )
        jumping = jnp.where((row_bit == 0) & (col_bit == 1), jnp.sqrt(damping[bit_pos]), 0.0)
        result = result * jnp.where(branches[bit_pos] == 0, staying, jumping)
    return result


def low_block(vector_pair, matrix):
    highest = lax.Precision.HIGHEST
    shaped = vector_pair.reshape(2, -1, 128)
    new_real = jnp.einsum("rj,kj->rk", shaped[0], matrix[0], precision=highest) - jnp.einsum(
        "rj,kj->rk", shaped[1], matrix[1], precision=highest
    )
    new_imag = jnp.einsum("rj,kj->rk", shaped[1], matrix[0], precision=highest) + jnp.einsum(
        "rj,kj->rk", shaped[0], matrix[1], precision=highest
    )
    return jnp.stack([new_real, new_imag]).reshape(vector_pair.shape)


def high_block(vector_pair, matrix):
    highest = lax.Precision.HIGHEST
    shaped = vector_pair.reshape(2, 128, -1)
    new_real = jnp.dot(matrix[0], shaped[0], precision=highest) - jnp.dot(
        matrix[1], shaped[1], precision=highest
    )
    new_imag = jnp.dot(matrix[0], shaped[1], precision=highest) + jnp.dot(
        matrix[1], shaped[0], precision=highest
    )
    return jnp.stack([new_real, new_imag]).reshape(vector_pair.shape)


def top_block(portion, matrix):
    highest = lax.Precision.HIGHEST
    groups = portion.shape[2]
    top_local = portion.shape[1]
    real_gate = matrix[0].reshape(groups, top_local, groups, top_local)
    imag_gate = matrix[1].reshape(groups, top_local, groups, top_local)
    new_real = jnp.einsum("pqgh,hgr->qpr", real_gate, portion[0], precision=highest) - jnp.einsum(
        "pqgh,hgr->qpr", imag_gate, portion[1], precision=highest
    )
    new_imag = jnp.einsum("pqgh,hgr->qpr", real_gate, portion[1], precision=highest) + jnp.einsum(
        "pqgh,hgr->qpr", imag_gate, portion[0], precision=highest
    )
    return jnp.stack([new_real, new_imag])


def through_top(blocked, work):
    return work(
        lax.all_to_all(blocked, ("gx", "gy", "gz"), split_axis=2, concat_axis=2, tiled=True)
    )


def outcome_match(group_number, width_bits, outcomes):
    matched = jnp.ones(group_number.shape, jnp.bool_)
    for which in range(4):
        matched = matched & (
            jnp.bitwise_and(jnp.right_shift(group_number, width_bits - 1 - which), 1)
            == outcomes[which]
        )
    return matched.astype(jnp.float32)


def collapse(vector_pair, selector, total_amps):
    kraus_total = lax.psum(jnp.sum(vector_pair * vector_pair), ("gx", "gy", "gz"))
    scaled = vector_pair * jnp.sqrt(total_amps / kraus_total)
    projected = scaled * selector
    kept_total = lax.psum(jnp.sum(projected * projected), ("gx", "gy", "gz"))
    probability = kept_total / total_amps
    return (projected / jnp.sqrt(probability), probability)


def shards(initial_state, local_gates, top_gates, placement, damping, branches, outcomes):
    amplitudes = initial_state.shape[-1]
    devices = lax.axis_size("gx") * lax.axis_size("gy") * lax.axis_size("gz")
    width_bits = devices.bit_length() - 1
    top_local = 128 // devices
    row_count = amplitudes // 128
    total_amps = float(amplitudes * devices)
    matrices = [
        oriented(local_gates[0], placement[0]),
        oriented(local_gates[1], placement[1]),
        oriented(top_gates[0], placement[2]),
        oriented(local_gates[2], placement[3]),
        oriented(top_gates[1], placement[4]),
    ]
    kraus = kraus_matrix(damping, branches)
    state_now = initial_state.reshape(2, amplitudes)
    state_now = low_block(state_now, matrices[0])
    state_now = high_block(state_now, matrices[1])
    blocked_shape = (2, top_local, devices, row_count)

    def lifted(matrix):

        def work(portion):
            return lax.all_to_all(
                top_block(portion, matrix),
                ("gx", "gy", "gz"),
                split_axis=2,
                concat_axis=2,
                tiled=True,
            )

        return work

    state_now = through_top(state_now.reshape(blocked_shape), lifted(matrices[2])).reshape(
        2, amplitudes
    )
    state_now = low_block(state_now, matrices[3])
    state_now = through_top(state_now.reshape(blocked_shape), lifted(matrices[4])).reshape(
        2, amplitudes
    )
    state_now = jnp.stack(
        [
            jnp.dot(
                state_now[part_index].reshape(-1, 128), kraus.T, precision=lax.Precision.HIGHEST
            ).reshape(amplitudes)
            for part_index in range(2)
        ]
    )
    device_index = (
        lax.axis_index("gx") * lax.axis_size("gy") + lax.axis_index("gy")
    ) * lax.axis_size("gz") + lax.axis_index("gz")
    selector = outcome_match(device_index, width_bits, outcomes)
    collapsed, probability = collapse(state_now, selector, total_amps)
    return (collapsed.reshape(initial_state.shape), probability)


def solution(mesh):
    return jax.shard_map(
        shards,
        mesh=mesh,
        in_specs=(P(None, "gx", "gy", "gz", None), P(), P(), P(), P(), P(), P()),
        out_specs=(P(None, "gx", "gy", "gz", None), P()),
        check_vma=False,
    )
```

profile of v0, /device:TPU:1, one launch (start us, length us, event | category | flops | bytes accessed | tf_op | source)
XLA Modules:
  0.0 283.2 jit_solution(16526214849896523003)
XLA Ops:
  0.6 2.0 fusion.98
  2.6 4.3 %shift-left_add_fusion.4 = s32[128]{0:T(128)S(1)} fusion(s32[]{:T(128)} %bitcast.6, s32[]{:T(128)} %bitcast.5, s32[]{:T(128)} %bitcast.4, s32[]{:T(128)} %bitcast.3, s32[]{:T(128)} %bitcast.2, s32[]{:T(128)} %bitcast.1, s32[]{:T(128)} %bitcast), kind=kLoop, calls=%fused_computation.125 | loop fusion | flops 3456 | bytes 540 | tf_op jit(solution)/shard_map/add | solution.py:12
  6.9 1.1 fusion.42
  8.0 1.1 fusion.48
  9.1 4.6 %shift-left_add_fusion.3 = s32[128]{0:T(128)S(1)} fusion(s32[]{:T(128)} %bitcast.14, s32[]{:T(128)} %bitcast.13, s32[]{:T(128)} %bitcast.12, s32[]{:T(128)} %bitcast.11, s32[]{:T(128)} %bitcast.10, s32[]{:T(128)} %bitcast.9, s32[]{:T(128)} %bitcast.8), kind=kLoop, calls=%fused_computation.124 | loop fusion | flops 3456 | bytes 540 | tf_op jit(solution)/shard_map/add | solution.py:12
  13.7 1.1 fusion.44
  14.8 1.1 fusion.46
  22.5 1.8 copy.17
  24.3 11.5 %all-to-all-start = ((f32[2,1,128,1024]{3,0,1,2:T(2,128)}), f32[2,1,128,1024]{3,0,1,2:T(2,128)S(1)}, u32[]{:S(2)}, u32[]{:S(2)}) async-start(f32[2,1,128,1024]{3,0,1,2:T(2,128)} %copy.17), calls=%async_computation | async-start | bytes 2097152 | tf_op jit(solution)/shard_map/all_to_all | solution.py:82
  35.9 0.6 copy-done.2
  36.5 0.7 fusion.97
  37.2 4.4 %shift-left_add_fusion.2 = s32[128]{0:T(128)S(1)} fusion(s32[]{:T(128)} %bitcast.31, s32[]{:T(128)} %bitcast.30, s32[]{:T(128)} %bitcast.29, s32[]{:T(128)} %bitcast.28, s32[]{:T(128)} %bitcast.27, s32[]{:T(128)} %bitcast.26, s32[]{:T(128)} %bitcast.25), kind=kLoop, calls=%fused_computation.123 | loop fusion | flops 3456 | bytes 540 | tf_op jit(solution)/shard_map/add | solution.py:12
  41.7 0.7 fusion.99
  43.4 11.7 %all-to-all-done = f32[2,1,128,1024]{3,0,1,2:T(2,128)S(1)} async-done(((f32[2,1,128,1024]{3,0,1,2:T(2,128)}), f32[2,1,128,1024]{3,0,1,2:T(2,128)S(1)}, u32[]{:S(2)}, u32[]{:S(2)}) %all-to-all-start) | async-done | bytes 1048608 | tf_op jit(solution)/shard_map/all_to_all | solution.py:82
  55.2 0.8 fusion.95
  56.0 1.0 fusion.20
  57.0 1.0 fusion.16
  58.0 1.0 fusion.3
  59.0 1.0 fusion.2
  60.1 1.9 copy.18
  62.0 4.6 %all-to-all-start.1 = ((f32[2,1,128,1024]{3,1,0,2:T(1,128)}), f32[2,1,128,1024]{3,1,0,2:T(1,128)S(1)}, u32[]{:S(2)}, u32[]{:S(2)}) async-start(f32[2,1,128,1024]{3,1,0,2:T(1,128)} %copy.18), calls=%async_computation.1 | async-start | bytes 2097152 | tf_op jit(solution)/shard_map/all_to_all | solution.py:128
  66.6 4.4 %shift-left_add_fusion.1 = s32[128]{0:T(128)S(1)} fusion(s32[]{:T(128)} %bitcast.47, s32[]{:T(128)} %bitcast.46, s32[]{:T(128)} %bitcast.45, s32[]{:T(128)} %bitcast.44, s32[]{:T(128)} %bitcast.43, s32[]{:T(128)} %bitcast.42, s32[]{:T(128)} %bitcast.41), kind=kLoop, calls=%fused_computation.122 | loop fusion | flops 3456 | bytes 540 | tf_op jit(solution)/shard_map/add | solution.py:12
  71.1 0.7 fusion.101
  71.7 1.1 fusion.34
  72.8 1.1 fusion.36
  74.4 11.7 %all-to-all-done.1 = f32[2,1,128,1024]{3,1,0,2:T(1,128)S(1)} async-done(((f32[2,1,128,1024]{3,1,0,2:T(1,128)}), f32[2,1,128,1024]{3,1,0,2:T(1,128)S(1)}, u32[]{:S(2)}, u32[]{:S(2)}) %all-to-all-start.1) | async-done | bytes 1048608 | tf_op jit(solution)/shard_map/all_to_all | solution.py:128
  86.1 0.7 fusion.94
  89.2 2.0 pad_maximum_fusion.1
  91.2 4.5 %all-to-all-start.2 = ((f32[2,1,128,1024]{3,1,0,2:T(1,128)}), f32[2,1,128,1024]{3,1,0,2:T(1,128)S(1)}, u32[]{:S(2)}, u32[]{:S(2)}) async-start(f32[2,1,128,1024]{3,1,0,2:T(1,128)} %pad_maximum_fusion.1), calls=%async_computation.2 | async-start | bytes 2097152 | tf_op jit(solution)/shard_map/all_to_all | solution.py:82
  95.7 4.3 %shift-left_add_fusion = s32[128]{0:T(128)S(1)} fusion(s32[]{:T(128)} %bitcast.59, s32[]{:T(128)} %bitcast.58, s32[]{:T(128)} %bitcast.57, s32[]{:T(128)} %bitcast.56, s32[]{:T(128)} %bitcast.55, s32[]{:T(128)} %bitcast.54, s32[]{:T(128)} %bitcast.53), kind=kLoop, calls=%fused_computation.121 | loop fusion | flops 3456 | bytes 540 | tf_op jit(solution)/shard_map/add | solution.py:12
  101.3 0.7 fusion.100
  103.0 12.2 %all-to-all-done.2 = f32[2,1,128,1024]{3,1,0,2:T(1,128)S(1)} async-done(((f32[2,1,128,1024]{3,1,0,2:T(1,128)}), f32[2,1,128,1024]{3,1,0,2:T(1,128)S(1)}, u32[]{:S(2)}, u32[]{:S(2)}) %all-to-all-start.2) | async-done | bytes 1048608 | tf_op jit(solution)/shard_map/all_to_all | solution.py:82
  115.2 0.7 fusion.93
  115.9 1.0 fusion.14
  116.9 1.0 fusion.10
  117.9 1.0 fusion.1
  118.9 1.0 fusion
  120.0 1.9 copy.21
  121.9 4.5 %all-to-all-start.3 = ((f32[2,1,128,1024]{3,1,0,2:T(1,128)}), f32[2,1,128,1024]{3,1,0,2:T(1,128)S(1)}, u32[]{:S(2)}, u32[]{:S(2)}) async-start(f32[2,1,128,1024]{3,1,0,2:T(1,128)} %copy.21), calls=%async_computation.3 | async-start | bytes 2097152 | tf_op jit(solution)/shard_map/all_to_all | solution.py:128
  141.9 4.0 %all-to-all-done.3 = f32[2,1,128,1024]{3,1,0,2:T(1,128)S(1)} async-done(((f32[2,1,128,1024]{3,1,0,2:T(1,128)}), f32[2,1,128,1024]{3,1,0,2:T(1,128)S(1)}, u32[]{:S(2)}, u32[]{:S(2)}) %all-to-all-start.3) | async-done | bytes 1048608 | tf_op jit(solution)/shard_map/all_to_all | solution.py:128
  145.9 0.7 fusion.92
  146.6 1.0 fusion.91
  147.7 1.0 fusion.90
  148.7 1.7 multiply_reduce_fusion.1
  150.4 63.7 %psum.14 = f32[]{:T(128)} all-reduce(f32[]{:T(128)} %multiply_reduce_fusion.1), channel_id=1, replica_groups=mesh['gx'=4,'gy'=4,'gz'=8] {'gx','gy','gz'}, use_global_device_ids=true, to_apply=%region_1.2 | all-reduce | flops 1 | bytes 8 | tf_op jit(solution)/shard_map/psum | solution.py:97
  214.8 2.0 multiply_reduce_fusion
  216.8 62.6 %psum.15 = f32[]{:T(128)} all-reduce(f32[]{:T(128)} %multiply_reduce_fusion), channel_id=1, replica_groups=mesh['gx'=4,'gy'=4,'gz'=8] {'gx','gy','gz'}, use_global_device_ids=true, to_apply=%region_3.4 | all-reduce | flops 1 | bytes 8 | tf_op jit(solution)/shard_map/psum | solution.py:100
  280.1 1.9 fusion.9
  (60 shorter events, 12.3 us)
Async XLA Ops:
  0.6 16.4 %copy-start = (f32[2,1,1,1,131072]{4,3,2,1,0:T(1,128)S(1)}, f32[2,1,1,1,131072]{4,3,2,1,0:T(1,128)}, u32[]{:S(2)}) copy-start(f32[2,1,1,1,131072]{4,3,2,1,0:T(1,128)} %param.7) | copy-start | bytes 3145732
  24.3 17.4 %copy-start.5 = (s32[4]{0:T(128)S(1)}, s32[4]{0:T(128)}, u32[]{:S(2)}) copy-start(s32[4]{0:T(128)} %param.13) | copy-start | bytes 52
  24.3 18.1 %copy-start.1 = (f32[2,2,128,128]{3,2,1,0:T(8,128)S(1)}, f32[2,2,128,128]{3,2,1,0:T(8,128)}, u32[]{:S(2)}) copy-start(f32[2,2,128,128]{3,2,1,0:T(8,128)} %param.9) | copy-start | bytes 786436
  24.3 30.9 %all-to-all-start = ((f32[2,1,128,1024]{3,0,1,2:T(2,128)}), f32[2,1,128,1024]{3,0,1,2:T(2,128)S(1)}, u32[]{:S(2)}, u32[]{:S(2)}) async-start(f32[2,1,128,1024]{3,0,1,2:T(2,128)} %copy.17), calls=%async_computation | async-start | bytes 2097152 | tf_op jit(solution)/shard_map/all_to_all | solution.py:82
  35.8 0.7 copy-start.2
  62.0 9.1 %copy-start.3 = (f32[7]{0:T(128)S(1)}, f32[7]{0:T(128)}, u32[]{:S(2)}) copy-start(f32[7]{0:T(128)} %param.11) | copy-start | bytes 88
  62.0 24.1 %all-to-all-start.1 = ((f32[2,1,128,1024]{3,1,0,2:T(1,128)}), f32[2,1,128,1024]{3,1,0,2:T(1,128)S(1)}, u32[]{:S(2)}, u32[]{:S(2)}) async-start(f32[2,1,128,1024]{3,1,0,2:T(1,128)} %copy.18), calls=%async_computation.1 | async-start | bytes 2097152 | tf_op jit(solution)/shard_map/all_to_all | solution.py:128
  91.2 24.0 %all-to-all-start.2 = ((f32[2,1,128,1024]{3,1,0,2:T(1,128)}), f32[2,1,128,1024]{3,1,0,2:T(1,128)S(1)}, u32[]{:S(2)}, u32[]{:S(2)}) async-start(f32[2,1,128,1024]{3,1,0,2:T(1,128)} %pad_maximum_fusion.1), calls=%async_computation.2 | async-start | bytes 2097152 | tf_op jit(solution)/shard_map/all_to_all | solution.py:82
  100.7 0.7 copy-start.4
  121.9 24.0 %all-to-all-start.3 = ((f32[2,1,128,1024]{3,1,0,2:T(1,128)}), f32[2,1,128,1024]{3,1,0,2:T(1,128)S(1)}, u32[]{:S(2)}, u32[]{:S(2)}) async-start(f32[2,1,128,1024]{3,1,0,2:T(1,128)} %copy.21), calls=%async_computation.3 | async-start | bytes 2097152 | tf_op jit(solution)/shard_map/all_to_all | solution.py:128
where the time goes:
time: 285 us; the launch traced here: 283 us
  blocking collectives  126 us (44%)
  waiting for transfers between devices  39.6 us (14%)
  other arithmetic  30 us (11%)
  matrix products  27.1 us (10%)
  starting transfers between devices  25.1 us (9%)
  between operations  19.9 us (7%)
  local copies, waits for them, and re-layouts  15.1 us (5%)
    psum x1, blocking collectives, collapse(): lax.psum(jnp.sum(vector_pair * vector_pair), ('gx', 'gy', 'gz'))  63.7 us
    psum x1, blocking collectives, collapse(): kept_total = lax.psum(jnp.sum(projected * projected), ('gx', 'gy', 'gz'))  62.6 us
    all_to_all x2, waiting for transfers between devices, through_top(): lax.all_to_all(blocked, ('gx', 'gy', 'gz'), split_axis=2, concat_axis=2,...  23.9 us
    add x5, other arithmetic, oriented(): source = source + jnp.left_shift(picked, bit_pos)  22.1 us
    all_to_all x2, starting transfers between devices, through_top(): lax.all_to_all(blocked, ('gx', 'gy', 'gz'), split_axis=2, concat_axis=2,...  16 us
    all_to_all x2, waiting for transfers between devices, work(): lax.all_to_all(top_block(portion, matrix), ('gx', 'gy', 'gz'), split_axis...  15.7 us
    all_to_all x2, starting transfers between devices, work(): lax.all_to_all(top_block(portion, matrix), ('gx', 'gy', 'gz'), split_axis...  9.13 us
    dot_general x10, matrix products, oriented(): jnp.dot(selector_matrix, gate[part_index], precision=highest)  7.33 us
  transfers between devices with their start and end apart: 4, of which 4 were waited for; matrix products, arithmetic and copies ran while one was open for 7% of the time, Pallas kernels for 0%

commit v1 on v0

v1 whole, which is shorter than its diff:
```python
import functools

import jax
import jax.numpy as jnp
from jax import lax
from jax.experimental import pallas as pl
from jax.experimental.pallas import tpu as pltpu
from jax.sharding import PartitionSpec as P

F32 = jnp.float32
BF16 = jnp.bfloat16
I32 = jnp.int32
MESH = pl.DeviceIdType.MESH
TOTAL = 16777216.0


def split(a):
    high = a.astype(BF16)
    return high, (a - high.astype(F32)).astype(BF16)


def mm(a, b, transposed=False):
    dims = (((1,), (1 if transposed else 0,)), ((), ()))
    return lax.dot_general(a, b, dims, preferred_element_type=F32)


def dot_split(a, b, transposed=False):
    return mm(a[0], b[0], transposed) + (mm(a[0], b[1], transposed) + mm(a[1], b[0], transposed))


def dot3(a, b, transposed=False):
    return dot_split(split(a), split(b), transposed)


def permuted_rows(onehot, b):
    high, low = split(b)
    return mm(onehot, high) + mm(onehot, low)


def permuted_columns(a, onehot):
    high, low = split(a)
    return mm(high, onehot) + mm(low, onehot)


def lanes(width=128):
    return lax.broadcasted_iota(I32, (1, width), 1)


def source(legs, k):
    out = jnp.zeros_like(k)
    for i in range(7):
        out = out | (((k >> legs[i]) & 1) << i)
    return out


def unsource(legs, s):
    out = jnp.zeros_like(s)
    for i in range(7):
        out = out | (((s >> i) & 1) << legs[i])
    return out


def hits(target, rows=128):
    return lax.broadcasted_iota(I32, (rows, target.shape[1]), 0) == target


def onehot(target, rows=128):
    return jnp.where(hits(target, rows), 1.0, 0.0).astype(BF16)


def compact_index(branches, j):
    out = jnp.zeros_like(j)
    count = jnp.int32(0)
    for i in range(7):
        stays = 1 - branches[i]
        out = out | ((((j >> i) & 1) * stays) << count)
        count = count + stays
    return out


def kraus_weight(branches, damping, j):
    weight = jnp.ones(j.shape, F32)
    for i in range(7):
        bit = ((j >> i) & 1) == 1
        d = jnp.full(j.shape, damping[i], F32)
        root = jnp.sqrt(jnp.where(branches[i] == 0, 1.0 - d, d))
        off = jnp.where(branches[i] == 0, 1.0, 0.0)
        weight = weight * jnp.where(bit, root, off)
    return weight


def complex_rows(pair):
    half = pair.shape[0] // 2
    r, i = pair[:half], pair[half:]
    return jnp.concatenate(
        [jnp.concatenate([r, -i], axis=1), jnp.concatenate([i, r], axis=1)], axis=0
    )


def complex_columns(pair):
    half = pair.shape[1] // 2
    r, i = pair[:, :half], pair[:, half:]
    return jnp.concatenate(
        [jnp.concatenate([r, i], axis=1), jnp.concatenate([-i, r], axis=1)], axis=0
    )


def side(gate_ref, which):
    return jnp.concatenate([gate_ref[which, 0], gate_ref[which, 1]], axis=1)


def stack_halves(pair):
    half = pair.shape[1] // 2
    return jnp.concatenate([pair[:, :half], pair[:, half:]], axis=0)


def side_halves(pair):
    half = pair.shape[0] // 2
    return jnp.concatenate([pair[:half], pair[half:]], axis=1)


HOPS = (0, 1, 2, 1)


def hops(offset):
    dy, dh, dz, dl = offset
    return HOPS[dy] + HOPS[dz] + (2 if (dh, dl) == (1, 0) else dh | dl)


CHIPS = [
    (dy, dh, dz, dl)
    for dy in range(4)
    for dh in range(2)
    for dz in range(4)
    for dl in range(2)
    if dy or dh or dz or dl
]
FAR = [sorted((o for o in CHIPS if hops(o) in at), key=hops, reverse=True) for at in ((6, 5), (4,))]
NEAR = [[o for o in CHIPS if hops(o) == at] for at in (3, 2, 1)]


def each_core(classes, act):
    for offsets in classes:

        @pl.loop(0, 2)
        def _(other, offsets=offsets):
            for offset in offsets:
                act(offset, other)


OWNERS = [
    (f, dh, dz, dl)
    for f in (1, 0)
    for dh in range(2)
    for dz in range(4)
    for dl in range(2)
    if f or dh or dz or dl
]
OWNER_CLASSES = [[o for o in OWNERS if hops(o) in at] for at in ((5,), (4,), (3,), (2,), (1,))]


def each_owner(place, act):
    each_core(OWNER_CLASSES, act)
    act((0, 0, 0, 0), 1)

    @pl.when(jnp.logical_not(place.owner))
    def _():
        act((0, 0, 0, 0), 0)


def each_other(act):
    each_core(FAR + NEAR, act)
    act((0, 0, 0, 0), 1)


class Place:
    def __init__(self):
        gx, gy, gz = (lax.axis_index(name) for name in ("gx", "gy", "gz"))
        self.index = (gx * 4 + gy) * 8 + gz
        self.row, self.column = gx * 4 + gy, gz
        self.core, xh = lax.rem(gy, 2), lax.div(gy, 2)
        z, xl = lax.div(gz, 2), lax.rem(gz, 2)
        self.ys = [gx] + [lax.rem(gx + d, 4) for d in (1, 2, 3)]
        zs = [z] + [lax.rem(z + d, 4) for d in (1, 2, 3)]
        self.owner = gx < 2
        near = lax.div(lax.rem(gx + 1, 4), 2)
        self.owner_ys = [near, 1 - near]
        self.xhs = [xh * 2, 2 - xh * 2]
        xls = [xl, 1 - xl]
        self.gzs = [[zs[dz] * 2 + xls[dl] for dl in range(2)] for dz in range(4)]

    def device(self, offset, other):
        dy, dh, dz, dl = offset
        core = self.core + other * (1 - 2 * self.core)
        return (self.ys[dy], self.xhs[dh] + core, self.gzs[dz][dl])

    def owner_device(self, offset, other):
        f, dh, dz, dl = offset
        core = self.core + other * (1 - 2 * self.core)
        return (self.owner_ys[f], self.xhs[dh] + core, self.gzs[dz][dl])

    def column_of(self, offset):
        return self.gzs[offset[2]][offset[3]]

    def index_of(self, offset, other):
        gx, gy, gz = self.device(offset, other)
        return (gx * 4 + gy) * 8 + gz


def block(ref, index, rows):
    return ref.at[pl.ds(index * rows, rows)]


def wait_for(ref, rows, sem):
    part = ref.at[pl.ds(0, rows)]
    pltpu.make_async_copy(part, part, sem).wait()


def layout(level):
    shared = level > 3
    return shared, 1 if shared else 2, max(8 >> level, 1), 128 >> level


def main_kernel(
    level,
    x_hbm,
    local_hbm,
    top_hbm,
    placement_hbm,
    damping_hbm,
    branches_hbm,
    outcomes_hbm,
    f_ref,
    packed_ref,
    chosen_ref,
    p_ref,
    x_ref,
    local_ref,
    top_ref,
    placement,
    damping,
    branches,
    outcomes,
    out_buf,
    in_buf,
    back_out,
    back_in,
    in_sem,
    send_sem,
    recv_sem,
    own_sem,
    ready_sem,
):
    shared, parts, groups, width = layout(level)
    per_block = 2 if shared else parts * groups
    per_back = per_block + 1
    place = Place()

    barrier = pltpu.get_barrier_semaphore()

    def enter(offset, other):
        pl.semaphore_signal(
            barrier, inc=1, device_id=place.device(offset, other), device_id_type=MESH
        )

    if shared:
        pl.when(place.owner)(lambda: each_other(enter))
    else:
        each_core(FAR, enter)
    loads = [
        pltpu.make_async_copy(src, dst, in_sem.at[n])
        for n, (src, dst) in enumerate(
            (
                (branches_hbm, branches),
                (damping_hbm, damping),
                (placement_hbm, placement),
                (outcomes_hbm, outcomes),
                (local_hbm, local_ref),
                (x_hbm, x_ref),
                (top_hbm, top_ref),
            )
        )
    ]
    for load in loads:
        load.start()
    if not shared:
        each_core(NEAR, enter)
        enter((0, 0, 0, 0), 1)
    for load in loads[:6]:
        load.wait()

    legs = [[placement[t, i] for i in range(7)] for t in range(5)]
    branch = [branches[i] for i in range(7)]
    damp = [damping[i] for i in range(7)]
    lane = lanes()

    after = unsource(legs[3], lane)
    left = jnp.where(
        hits(compact_index(branch, after), width), kraus_weight(branch, damp, after), 0.0
    )
    left = dot3(left, side(local_ref, 2))
    right = permuted_rows(
        onehot(source(legs[3], unsource(legs[0], lane))), side(local_ref, 0)
    )
    right = permuted_columns(stack_halves(right), onehot(source(legs[0], lane)))
    low = stack_halves(dot3(left, complex_columns(side_halves(right))))
    low = split(complex_rows(low))

    mid = permuted_rows(onehot(unsource(legs[1], lane)), side(local_ref, 1))
    mid = permuted_columns(stack_halves(mid), onehot(source(legs[1], lane)))
    mid = complex_rows(mid)
    mid = split(mid[:128] if shared else mid)

    rows = jnp.concatenate(
        [
            jnp.concatenate(
                [x_ref[pl.ds(q, 128, stride=8), :], x_ref[pl.ds(1024 + q, 128, stride=8), :]], axis=1
            )
            for q in range(8)
        ],
        axis=0,
    )
    z = dot_split(low, split(rows), transposed=True)
    for g in range(groups):
        pieces, turned = [], []
        for u in range(8 // groups):
            q = g * (8 // groups) + u
            piece = z[:, q * 128 : q * 128 + 128]
            r, i = piece[:width], piece[width:]
            pieces.append(jnp.concatenate([r, i], axis=1))
            turned.append(jnp.concatenate([i, -r], axis=1))
        if shared:
            pieces = pieces + turned
        y = dot_split(mid, split(jnp.concatenate(pieces, axis=0)), transposed=True)
        if shared:
            for block_of in range(2):
                out_buf[pl.ds(block_of, 64, stride=2), :] = y[block_of * 64 : block_of * 64 + 64]
            continue
        for part in range(parts):
            out_buf[pl.ds(part * groups + g, 128, stride=per_block), :] = y[
                part * 128 : part * 128 + 128
            ]

    if shared:
        pl.when(place.owner)(lambda: pl.semaphore_wait(barrier, 63))
        pl.when(jnp.logical_not(place.owner))(lambda: pl.semaphore_wait(barrier, 64))
    else:
        pl.semaphore_wait(barrier, 127)

    def send(offset, other):
        pltpu.make_async_remote_copy(
            src_ref=block(out_buf, place.index_of(offset, other), per_block),
            dst_ref=block(in_buf, place.index, per_block),
            send_sem=send_sem.at[0],
            recv_sem=recv_sem.at[0],
            device_id=place.device(offset, other),
            device_id_type=MESH,
        ).start()

    own = pltpu.make_async_copy(
        block(out_buf, place.index, per_block), block(in_buf, place.index, per_block), own_sem.at[0]
    )

    def send_owner(offset, other):
        gx, gy, gz = device = place.owner_device(offset, other)
        pltpu.make_async_remote_copy(
            src_ref=block(out_buf, (gx * 4 + gy) * 8 + gz, 2),
            dst_ref=block(in_buf, place.index, 2),
            send_sem=send_sem.at[0],
            recv_sem=recv_sem.at[0],
            device_id=device,
            device_id_type=MESH,
        ).start()

    def tell_owner(offset, other):
        pl.semaphore_signal(
            ready_sem, inc=1, device_id=place.owner_device(offset, other), device_id_type=MESH
        )

    if shared:
        each_owner(place, send_owner)
        pl.when(jnp.logical_not(place.owner))(lambda: each_owner(place, tell_owner))
    else:
        each_other(send)
        own.start()

    loads[6].wait()
    zero_row = jnp.zeros_like(lane)
    for n in range(7):
        zero_row = zero_row | (((lane >> n) & 1) * branch[n])
    packed_ref[...] = jnp.where(zero_row == 0, compact_index(branch, lane), -1)

    top = permuted_rows(onehot(unsource(legs[4], lane)), side(top_ref, 1))
    top = permuted_columns(
        stack_halves(top), onehot(source(legs[4], unsource(legs[2], lane)))
    )
    top = dot3(side_halves(top), complex_columns(side(top_ref, 0)))
    top = permuted_columns(stack_halves(top), onehot(source(legs[2], lane)))
    top = split(side_halves(top) if shared else complex_rows(top))
    chosen = outcomes[0] * 8 + outcomes[1] * 4 + outcomes[2] * 2 + outcomes[3]

    first_half = lane < 64

    def send_back(offset, other):
        pltpu.make_async_remote_copy(
            src_ref=block(back_out, place.column_of(offset), per_back),
            dst_ref=block(back_in, place.index, per_back),
            send_sem=send_sem.at[1],
            recv_sem=recv_sem.at[1],
            device_id=place.device(offset, other),
            device_id_type=MESH,
        ).start()

    own_back = pltpu.make_async_copy(
        block(back_out, place.column, per_back), block(back_in, place.index, per_back), own_sem.at[1]
    )

    def fold(norm, kept):
        return jnp.where(
            first_half, norm + pltpu.roll(norm, 64, axis=1), kept + pltpu.roll(kept, 64, axis=1)
        )

    def finish(sums, rows):
        sums = jnp.sum(sums, axis=0, keepdims=True)
        norm = jnp.sum(jnp.where(first_half, sums, 0.0), keepdims=True)
        kept = jnp.sum(jnp.where(first_half, 0.0, sums), keepdims=True)
        probability = kept / norm
        scale = jnp.sqrt(TOTAL / norm) / jnp.sqrt(probability)
        for part, first, count, start, value in rows:
            f_ref[part, pl.ds(first, count), pl.ds(start, 128)] = value * scale
        p_ref[0] = jnp.max(probability)
        chosen_ref[0] = jnp.where(chosen == place.row, 1, 0) + jnp.where(p_ref[0] > 0.0, 0, 2)

    if shared:

        @pl.when(place.owner)
        def _():
            own.start()
            own.wait()
            wait_for(in_buf, 127 * 2, recv_sem.at[0])
            columns = []
            for block_of in range(2):
                b = in_buf[pl.ds(block_of, 128, stride=2), :]
                swapped = pltpu.roll(b, 64, axis=1)
                columns.append(
                    jnp.concatenate([b, jnp.where(first_half, -swapped, swapped)], axis=0)
                )
            psi = dot_split(top, split(jnp.concatenate(columns, axis=1)))
            norm = jnp.sum(psi * psi, axis=0, keepdims=True)
            picked = jnp.zeros((8, 256), F32)
            for group in range(16):
                picked = picked + jnp.where(chosen == group, psi[group * 8 : group * 8 + 8], 0.0)
            kept = jnp.sum(picked * picked, axis=0, keepdims=True)
            for block_of in range(2):
                back_out[pl.ds(block_of, 8, stride=3), :] = picked[
                    :, block_of * 128 : block_of * 128 + 128
                ]
            sums = fold(norm[:, :128] + norm[:, 128:], kept[:, :128] + kept[:, 128:])
            back_out[pl.ds(2, 8, stride=3), :] = jnp.broadcast_to(sums, (8, 128))
            pl.semaphore_wait(ready_sem, 64)
            each_other(send_back)
            own_back.start()
            own_back.wait()
            wait_for(back_in, 63 * 3, recv_sem.at[1])

        @pl.when(jnp.logical_not(place.owner))
        def _():
            wait_for(back_in, 64 * 3, recv_sem.at[1])

        finish(
            back_in[pl.ds(2, 64, stride=3), :],
            [(0, n * 64, 64, 0, back_in[pl.ds(n, 64, stride=3), :]) for n in range(2)],
        )

        @pl.when(place.owner)
        def _():
            wait_for(out_buf, 63 * 2, send_sem.at[0])
            wait_for(x_ref, 127 * 3, send_sem.at[1])

        @pl.when(jnp.logical_not(place.owner))
        def _():
            wait_for(out_buf, 64 * 2, send_sem.at[0])

        return

    own.wait()
    wait_for(in_buf, 127 * per_block, recv_sem.at[0])
    norm = jnp.zeros((1, 128), F32)
    kept = jnp.zeros((1, 128), F32)
    for g in range(groups):
        b = [in_buf[pl.ds(part * groups + g, 128, stride=per_block), :] for part in range(parts)]
        psi = dot_split(top, split(jnp.concatenate(b, axis=0)))
        norm = norm + jnp.sum(psi * psi, axis=0, keepdims=True)
        for part in range(parts):
            picked = jnp.zeros((8, 128), F32)
            for group in range(16):
                at = part * 128 + group * 8
                picked = picked + jnp.where(chosen == group, psi[at : at + 8], 0.0)
            kept = kept + jnp.sum(picked * picked, axis=0, keepdims=True)
            back_out[pl.ds(part * groups + g, 8, stride=per_back), :] = picked
    back_out[pl.ds(per_block, 8, stride=per_back), :] = jnp.broadcast_to(fold(norm, kept), (8, 128))
    each_other(send_back)
    own_back.start()
    own_back.wait()
    wait_for(back_in, 127 * per_back, recv_sem.at[1])
    finish(
        back_in[pl.ds(per_block, 128, stride=per_back), :],
        [
            (part, 0, 128, g * 128, back_in[pl.ds(part * groups + g, 128, stride=per_back), :])
            for part in range(parts)
            for g in range(groups)
        ],
    )
    wait_for(out_buf, 127 * per_block, send_sem.at[0])
    wait_for(back_in, 127 * per_back, send_sem.at[1])


def fill_rows(values, out_hbm, sems, first):
    copies = [
        pltpu.make_async_copy(
            values.at[pl.ds(0, 256)], out_hbm.at[pl.ds(first + n * 256, 256)], sems.at[n]
        )
        for n in range(4)
    ]
    for copy in copies:
        copy.start()
    for copy in copies:
        copy.wait()


def expand_kernel(
    level, chosen_ref, p_ref, f_ref, packed_ref, zeros_hbm, out_hbm, p_hbm, buf, sems
):
    shared, parts, groups, width = layout(level)
    each = 8 // groups
    p_copy = pltpu.make_async_copy(p_ref, p_hbm, sems.at[4])
    p_copy.start()
    state = chosen_ref[0]

    @pl.when(lax.rem(state, 2) == 1)
    def _():
        packed = packed_ref[...]
        copies = []
        for part in range(2):
            start = part * 64 if shared else 0
            tables = [
                onehot(jnp.where(packed >= 0, packed + start + u * width, -1)) for u in range(each)
            ]
            for g in range(groups):
                high, low = split(f_ref[part % parts, :, pl.ds(g * 128, 128)])
                for u, table in enumerate(tables):
                    q = g * each + u
                    buf[pl.ds(part * 1024 + q, 128, stride=8), :] = mm(high, table) + mm(low, table)
            here = pl.ds(part * 1024, 1024)
            copies.append(pltpu.make_async_copy(buf.at[here], out_hbm.at[here], sems.at[part]))
            copies[-1].start()
        for copy in copies:
            copy.wait()

    @pl.when(state == 0)
    def _():
        buf[pl.ds(0, 256), :] = jnp.zeros((256, 128), F32)
        fill_rows(buf, out_hbm, sems, 1024)

    @pl.when(state == 2)
    def _():
        buf[...] = jnp.full((2048, 128), jnp.nan, F32)
        copy = pltpu.make_async_copy(buf, out_hbm, sems.at[0])
        copy.start()
        copy.wait()

    p_copy.wait()


def run_level(level, buffer, x, local_gates, top_gates, placement, damping, branches, outcomes):
    shared, parts, groups, _ = layout(level)
    per_block = 2 if shared else parts * groups
    per_back = per_block + 1
    owners = 64 if shared else 128
    vmem = pl.BlockSpec(memory_space=pltpu.VMEM)
    hbm = pl.BlockSpec(memory_space=pltpu.HBM)
    smem = pl.BlockSpec(memory_space=pltpu.SMEM)
    packed, rows, chosen, probability = pl.pallas_call(
        functools.partial(main_kernel, level),
        out_shape=(
            pltpu.VMEM((parts, 128, 128 * groups), F32),
            pltpu.VMEM((1, 128), I32),
            pltpu.SMEM((1,), I32),
            pltpu.SMEM((1,), F32),
        ),
        in_specs=[hbm] * 7,
        out_specs=(vmem, vmem, smem, smem),
        scratch_shapes=[
            pltpu.VMEM((2048, 128), F32),
            pltpu.VMEM(local_gates.shape, F32),
            pltpu.VMEM(top_gates.shape, F32),
            pltpu.SMEM(placement.shape, I32),
            pltpu.SMEM(damping.shape, F32),
            pltpu.SMEM(branches.shape, I32),
            pltpu.SMEM(outcomes.shape, I32),
            pltpu.VMEM((owners * per_block, 128), F32),
            pltpu.VMEM((128 * per_block, 128), F32),
            pltpu.VMEM((8 * per_back, 128), F32),
            pltpu.VMEM((owners * per_back, 128), F32),
            pltpu.SemaphoreType.DMA((7,)),
            pltpu.SemaphoreType.DMA((2,)),
            pltpu.SemaphoreType.DMA((2,)),
            pltpu.SemaphoreType.DMA((2,)),
            pltpu.SemaphoreType.REGULAR,
        ],
        compiler_params=pltpu.CompilerParams(
            collective_id=level + 1, has_side_effects=True, vmem_limit_bytes=32 * 1024 * 1024
        ),
        name=f"window{level}",
    )(
        x,
        local_gates,
        top_gates,
        *(
            pltpu.with_memory_space_constraint(small, pltpu.HBM)
            for small in (placement, damping, branches, outcomes)
        ),
    )
    return pl.pallas_call(
        functools.partial(expand_kernel, level),
        out_shape=(
            pltpu.HBM((2048, 128), F32),
            pltpu.HBM((1,), F32),
        ),
        in_specs=[smem, smem, vmem, vmem, hbm],
        out_specs=(hbm, hbm),
        input_output_aliases={4: 0},
        scratch_shapes=[pltpu.VMEM((2048, 128), F32), pltpu.SemaphoreType.DMA((5,))],
        compiler_params=pltpu.CompilerParams(vmem_limit_bytes=32 * 1024 * 1024),
        name=f"expand{level}",
    )(
        chosen,
        probability,
        packed,
        rows,
        pltpu.with_memory_space_constraint(buffer, pltpu.HBM),
    )


def level_kernel(branches_hbm, *rest):
    *choice_refs, out_hbm, branches, zeros, sem, sems = rest
    load = pltpu.make_async_copy(branches_hbm, branches, sem)
    load.start()
    zeros[...] = jnp.zeros((256, 128), F32)
    fill_rows(zeros, out_hbm, sems, 0)
    load.wait()
    jumps = branches[0]
    for i in range(1, 7):
        jumps = jumps + branches[i]
    for limit, choice_ref in enumerate(choice_refs):
        choice_ref[0] = jnp.where(jumps > limit, 1, 0)


def choose_level(branches):
    return pl.pallas_call(
        level_kernel,
        out_shape=(pltpu.SMEM((1,), I32),) * 4 + (pltpu.HBM((2048, 128), F32),),
        in_specs=[pl.BlockSpec(memory_space=pltpu.HBM)],
        out_specs=(pl.BlockSpec(memory_space=pltpu.SMEM),) * 4
        + (pl.BlockSpec(memory_space=pltpu.HBM),),
        scratch_shapes=[
            pltpu.SMEM((7,), I32),
            pltpu.VMEM((256, 128), F32),
            pltpu.SemaphoreType.DMA,
            pltpu.SemaphoreType.DMA((4,)),
        ],
        name="level",
    )(branches)


def shards(initial_state, *small):
    *more, buffer = choose_level(small[4])
    level = [functools.partial(run_level, n) for n in range(5)]

    def either(choice, otherwise, then):
        return lambda choices, *args: lax.switch(
            choices[choice][0],
            [lambda _, *a: otherwise(*a), lambda _, *a: then(*a)],
            None,
            *args,
        )

    def two(choice, low, high):
        return lambda choices, *args: lax.switch(
            choices[choice][0],
            [lambda c, *a: low(c, *a), lambda c, *a: high(c, *a)],
            choices,
            *args,
        )

    tree = two(2, two(1, either(0, level[0], level[1]), lambda c, *a: level[2](*a)), either(3, level[3], level[4]))
    collapsed, probability = lax.optimization_barrier(
        tree(tuple(more), buffer, initial_state.reshape(2048, 128), *small)
    )
    return collapsed.reshape(initial_state.shape), probability.reshape(())


def solution(mesh):
    return jax.shard_map(
        shards,
        mesh=mesh,
        in_specs=(P(None, "gx", "gy", "gz", None), P(), P(), P(), P(), P(), P()),
        out_specs=(P(None, "gx", "gy", "gz", None), P()),
        check_vma=False,
    )
```

time: 285 us -> 24.7 us (0.09)
  blocking collectives: 126 us -> 0 us
  waiting for transfers between devices: 39.6 us -> 0 us
  other arithmetic: 30 us -> 0 us
  matrix products: 27.1 us -> 0 us
  starting transfers between devices: 25.1 us -> 0 us
  Pallas kernels: 0 us -> 23.5 us
  between operations: 19.9 us -> 0.82 us
  local copies, waits for them, and re-layouts: 15.1 us -> 0 us
    psum x2 -> x0, blocking collectives: 126 us -> none  [the longest x1 63.7 us: collapse(): lax.psum(jnp.sum(vector_pair * vector_pair), ('gx', 'gy', 'gz'))]
    all_to_all x4 -> x0, waiting for transfers between devices: 39.6 us -> none  [the longest x2 23.9 us: through_top(): lax.all_to_all(blocked, ('gx', 'gy', 'gz'), split_axis=2, concat_axis=2,...]
    dot_general x42 -> x0, matrix products: 27.1 us -> none  [the longest x10 7.33 us: oriented(): jnp.dot(selector_matrix, gate[part_index], precision=highest)]
    all_to_all x4 -> x0, starting transfers between devices: 25.1 us -> none  [the longest x2 16 us: through_top(): lax.all_to_all(blocked, ('gx', 'gy', 'gz'), split_axis=2, concat_axis=2,...]
    pallas_call x0 -> x3, Pallas kernels: none -> 23.5 us  [the longest x1 21.8 us: run_level(): pl.pallas_call(functools.partial(main_kernel, level), out_shape=(pltpu.VM...]
    add x5 -> x0, other arithmetic: 22.1 us -> none  [oriented(): source = source + jnp.left_shift(picked, bit_pos)]
    slice x10 -> x0, local copies, waits for them, and re-layouts: 7.74 us -> none  [the longest x2 2.7 us: oriented(): picked = jnp.bitwise_and(jnp.right_shift(lanes, leg_order[bit_pos]), 1)]
    another operation x3 -> x0, local copies, waits for them, and re-layouts: 5.58 us -> none  [the longest x2 3.8 us: top_block(): return jnp.stack([new_real, new_imag])]
  transfers between devices with their start and end apart: 4 -> 0, of which waited for: 4 -> 0; matrix products, arithmetic and copies ran while one was open for 7% -> 0% of each run, Pallas kernels for 0% -> 0%
where the time goes in v1:
time: 24.7 us; the launch traced here: 24.6 us
  Pallas kernels  23.5 us (95%)
  between operations  0.82 us (3%)
  loops' own time  0.28 us (1%)
    pallas_call x1, Pallas kernels, run_level(): pl.pallas_call(functools.partial(main_kernel, level), out_shape=(pltpu.VM...  21.8 us
    pallas_call x1, Pallas kernels, run_level(): pl.pallas_call(functools.partial(expand_kernel, level), out_shape=(pltpu....  0.86 us
    pallas_call x1, Pallas kernels, choose_level(): pl.pallas_call(level_kernel, out_shape=(pltpu.SMEM((1,), I32),) * 4 + (pl...  0.86 us

profile of v1, /device:TPU:1, one launch (start us, length us, event | category | flops | bytes accessed | tf_op | source)
XLA Modules:
  0.0 24.6 jit_solution(18103066386913556726)
XLA Ops:
  0.6 0.9 %level.1 = (s32[1]{0:T(128)S(4)}, s32[1]{0:T(128)S(4)}, s32[1]{0:T(128)S(4)}, s32[1]{0:T(128)S(4)}, f32[2048,128]{1,0:T(8,128)}) custom-call(s32[7]{0:T(128)} %branches_hbm.1), custom_call_target="tpu_custom_call" | custom-call | tf_op jit(solution)/shard_map/level/pallas_call | solution.py:660
  1.5 22.9 %conditional.4 = ((f32[2048,128]{1,0:T(8,128)}, f32[1]{0:T(128)})) conditional(s32[]{:T(128)} %bitcast.3, (s32[1]{0:T(128)S(4)}, s32[1]{0:T(128)S(4)}, f32[2048,128]{1,0:T(8,128)}, f32[3,2,128,128]{3,2,1,0:T(8,128)}, f32[2,2,128,128]{3,2,1,0:T(8,128)}, /*index=5*/s32[5,7]{1,0:T(8,128)}, f32[7]{0:T(128)}, s32[7]{0:T(128)}, s32[4]{0:T(128)}, ...), branch_computations={%region_0.0_spmd, %region_5.0_spmd} | conditional | flops 2 | bytes 240 | solution.py:689
  1.7 22.6 %conditional.2 = ((f32[2048,128]{1,0:T(8,128)}, f32[1]{0:T(128)})) conditional(s32[]{:T(128)} %bitcast.2, (f32[2048,128]{1,0:T(8,128)}, f32[3,2,128,128]{3,2,1,0:T(8,128)}, f32[2,2,128,128]{3,2,1,0:T(8,128)}, s32[5,7]{1,0:T(8,128)}, f32[7]{0:T(128)}, /*index=5*/s32[7]{0:T(128)}, s32[4]{0:T(128)}, f32[2048,128]{1,0:T(8,128)}) %tuple.26, ...), branch_computations={%region_6.0_spmd, %region_7.0_spmd} | conditional | bytes 8 | solution.py:681
  1.8 21.8 %window4.1 = (f32[1,128,128]{2,1,0:T(8,128)S(1)}, s32[1,128]{1,0:T(1,128)S(1)}, s32[1]{0:T(128)S(4)}, f32[1]{0:T(128)S(4)}) custom-call(f32[2048,128]{1,0:T(8,128)} %get-tuple-element.203.x_hbm, f32[3,2,128,128]{3,2,1,0:T(8,128)} %get-tuple-element.204.local_hbm, f32[2,2,128,128]{3,2,1,0:T(8,128)} %get-tuple-element.205.top_hbm, ...), custom_call_target="tpu_custom_call" | custom-call | tf_op jit(solution)/shard_map/cond/branch_1_fun/cond/branch_1_fun/window4/pallas_call | solution.py:583
  23.5 0.9 %expand4.1 = (f32[2048,128]{1,0:T(8,128)}, f32[1]{0:T(128)}) custom-call(s32[1]{0:T(128)S(4)} %get-tuple-element.210.chosen_ref, f32[1]{0:T(128)S(4)} %get-tuple-element.211.p_ref, f32[1,128,128]{2,1,0:T(8,128)S(1)} %get-tuple-element.212.f_ref, s32[1,128]{1,0:T(1,128)S(1)} %get-tuple-element.213.packed_ref, ...), custom_call_target="tpu_custom_call", output_to_operand_aliasing={{0}: (4, {})} | custom-call | tf_op jit(solution)/shard_map/cond/branch_1_fun/cond/branch_1_fun/expand4/pallas_call | solution.py:624

commit v2 on v1

--- a/solution.py
+++ b/solution.py
@@ -149,12 +149,12 @@
 
 
 OWNERS = [
-    (f, dh, dz, dl)
-    for f in (1, 0)
+    (dy, dh, f, dl)
+    for dy in range(4)
     for dh in range(2)
-    for dz in range(4)
+    for f in range(2)
     for dl in range(2)
-    if f or dh or dz or dl
+    if dy or dh or f or dl
 ]
 OWNER_CLASSES = [[o for o in OWNERS if hops(o) in at] for at in ((5,), (4,), (3,), (2,), (1,))]
 
@@ -182,12 +182,14 @@
         z, xl = lax.div(gz, 2), lax.rem(gz, 2)
         self.ys = [gx] + [lax.rem(gx + d, 4) for d in (1, 2, 3)]
         zs = [z] + [lax.rem(z + d, 4) for d in (1, 2, 3)]
-        self.owner = gx < 2
-        near = lax.div(lax.rem(gx + 1, 4), 2)
-        self.owner_ys = [near, 1 - near]
+        self.owner = gz < 4
+        self.owner_index = self.row * 4 + gz
+        near = lax.div(lax.rem(z + 1, 4), 2)
+        owner_zs = [near, 1 - near]
         self.xhs = [xh * 2, 2 - xh * 2]
         xls = [xl, 1 - xl]
         self.gzs = [[zs[dz] * 2 + xls[dl] for dl in range(2)] for dz in range(4)]
+        self.owner_gzs = [[owner_zs[f] * 2 + xls[dl] for dl in range(2)] for f in range(2)]
 
     def device(self, offset, other):
         dy, dh, dz, dl = offset
@@ -195,9 +197,9 @@
         return (self.ys[dy], self.xhs[dh] + core, self.gzs[dz][dl])
 
     def owner_device(self, offset, other):
-        f, dh, dz, dl = offset
+        dy, dh, f, dl = offset
         core = self.core + other * (1 - 2 * self.core)
-        return (self.owner_ys[f], self.xhs[dh] + core, self.gzs[dz][dl])
+        return (self.ys[dy], self.xhs[dh] + core, self.owner_gzs[f][dl])
 
     def column_of(self, offset):
         return self.gzs[offset[2]][offset[3]]
@@ -306,7 +308,10 @@
     low = stack_halves(dot3(left, complex_columns(side_halves(right))))
     low = split(complex_rows(low))
 
-    mid = permuted_rows(onehot(unsource(legs[1], lane)), side(local_ref, 1))
+    middle = unsource(legs[1], lane)
+    if shared:
+        middle = ((middle >> 2) & 1) * 64 + (middle >> 3) * 4 + (middle & 3)
+    mid = permuted_rows(onehot(middle), side(local_ref, 1))
     mid = permuted_columns(stack_halves(mid), onehot(source(legs[1], lane)))
     mid = complex_rows(mid)
     mid = split(mid[:128] if shared else mid)
@@ -357,14 +362,15 @@
             device_id_type=MESH,
         ).start()
 
+    slot = place.owner_index if shared else place.index
     own = pltpu.make_async_copy(
-        block(out_buf, place.index, per_block), block(in_buf, place.index, per_block), own_sem.at[0]
+        block(out_buf, slot, per_block), block(in_buf, place.index, per_block), own_sem.at[0]
     )
 
     def send_owner(offset, other):
         gx, gy, gz = device = place.owner_device(offset, other)
         pltpu.make_async_remote_copy(
-            src_ref=block(out_buf, (gx * 4 + gy) * 8 + gz, 2),
+            src_ref=block(out_buf, (gx * 4 + gy) * 4 + gz, 2),
             dst_ref=block(in_buf, place.index, 2),
             send_sem=send_sem.at[0],
             recv_sem=recv_sem.at[0],
@@ -404,7 +410,7 @@
     def send_back(offset, other):
         pltpu.make_async_remote_copy(
             src_ref=block(back_out, place.column_of(offset), per_back),
-            dst_ref=block(back_in, place.index, per_back),
+            dst_ref=block(back_in, slot, per_back),
             send_sem=send_sem.at[1],
             recv_sem=recv_sem.at[1],
             device_id=place.device(offset, other),
@@ -412,7 +418,7 @@
         ).start()
 
     own_back = pltpu.make_async_copy(
-        block(back_out, place.column, per_back), block(back_in, place.index, per_back), own_sem.at[1]
+        block(back_out, place.column, per_back), block(back_in, slot, per_back), own_sem.at[1]
     )
 
     def fold(norm, kept):
@@ -548,6 +554,11 @@
             ]
             for g in range(groups):
                 high, low = split(f_ref[part % parts, :, pl.ds(g * 128, 128)])
+                if shared:
+                    lane = lanes()
+                    owner = lane & 63
+                    order = onehot((owner >> 2) * 8 + (lane >> 6) * 4 + (owner & 3))
+                    high, low = mm(order, high).astype(BF16), mm(order, low).astype(BF16)
                 for u, table in enumerate(tables):
                     q = g * each + u
                     buf[pl.ds(part * 1024 + q, 128, stride=8), :] = mm(high, table) + mm(low, table)

time: 24.7 us -> 28.4 us (1.15)
  Pallas kernels: 23.5 us -> 26.6 us
  loops' own time: 0.28 us -> 0.77 us
    pallas_call x1, Pallas kernels: 21.8 us -> 24.9 us  [run_level(): pl.pallas_call(functools.partial(main_kernel, level), out_shape=(pltpu.VM...]
    another operation x1 -> x2, loops' own time: 0.25 us -> 0.77 us  [two(): lax.switch(choices[choice][0], [lambda c, *a: low(c, *a), lambda c, *a: h...]
where the time goes in v2:
time: 28.4 us; the launch traced here: 28.2 us
  Pallas kernels  26.6 us (94%)
  between operations  0.82 us (3%)
  loops' own time  0.77 us (3%)
    pallas_call x1, Pallas kernels, run_level(): pl.pallas_call(functools.partial(main_kernel, level), out_shape=(pltpu.VM...  24.9 us
    pallas_call x1, Pallas kernels, run_level(): pl.pallas_call(functools.partial(expand_kernel, level), out_shape=(pltpu....  0.86 us
    pallas_call x1, Pallas kernels, choose_level(): pl.pallas_call(level_kernel, out_shape=(pltpu.SMEM((1,), I32),) * 4 + (pl...  0.86 us
    another operation x2, loops' own time, two(): lax.switch(choices[choice][0], [lambda c, *a: low(c, *a), lambda c, *a: h...  0.77 us

profile of v2, /device:TPU:1, one launch (start us, length us, event | category | flops | bytes accessed | tf_op | source)
XLA Modules:
  0.0 28.2 jit_solution(363537813355834190)
XLA Ops:
  0.6 0.9 %level.1 = (s32[1]{0:T(128)S(4)}, s32[1]{0:T(128)S(4)}, s32[1]{0:T(128)S(4)}, s32[1]{0:T(128)S(4)}, f32[2048,128]{1,0:T(8,128)}) custom-call(s32[7]{0:T(128)} %branches_hbm.1), custom_call_target="tpu_custom_call" | custom-call | tf_op jit(solution)/shard_map/level/pallas_call | solution.py:671
  1.5 26.6 %conditional.4 = ((f32[2048,128]{1,0:T(8,128)}, f32[1]{0:T(128)})) conditional(s32[]{:T(128)} %bitcast.3, (s32[1]{0:T(128)S(4)}, s32[1]{0:T(128)S(4)}, f32[2048,128]{1,0:T(8,128)}, f32[3,2,128,128]{3,2,1,0:T(8,128)}, f32[2,2,128,128]{3,2,1,0:T(8,128)}, /*index=5*/s32[5,7]{1,0:T(8,128)}, f32[7]{0:T(128)}, s32[7]{0:T(128)}, s32[4]{0:T(128)}, ...), branch_computations={%region_0.0_spmd, %region_5.0_spmd} | conditional | flops 2 | bytes 240 | solution.py:700
  1.5 26.3 %conditional.1 = ((f32[2048,128]{1,0:T(8,128)}, f32[1]{0:T(128)})) conditional(s32[]{:T(128)} %bitcast.1, (s32[1]{0:T(128)S(4)}, f32[2048,128]{1,0:T(8,128)}, f32[3,2,128,128]{3,2,1,0:T(8,128)}, f32[2,2,128,128]{3,2,1,0:T(8,128)}, s32[5,7]{1,0:T(8,128)}, /*index=5*/f32[7]{0:T(128)}, s32[7]{0:T(128)}, s32[4]{0:T(128)}, ...), branch_computations={%region_1.0_spmd, %region_4.0_spmd} | conditional | flops 1 | bytes 88 | solution.py:700
  1.8 24.9 %window2.1 = (f32[2,128,256]{2,1,0:T(8,128)S(1)}, s32[1,128]{1,0:T(1,128)S(1)}, s32[1]{0:T(128)S(4)}, f32[1]{0:T(128)S(4)}) custom-call(f32[2048,128]{1,0:T(8,128)} %get-tuple-element.169.x_hbm, f32[3,2,128,128]{3,2,1,0:T(8,128)} %get-tuple-element.170.local_hbm, f32[2,2,128,128]{3,2,1,0:T(8,128)} %get-tuple-element.171.top_hbm, ...), custom_call_target="tpu_custom_call" | custom-call | tf_op jit(solution)/shard_map/cond/branch_0_fun/cond/branch_1_fun/window2/pallas_call | solution.py:594
  26.7 0.9 %expand2.1 = (f32[2048,128]{1,0:T(8,128)}, f32[1]{0:T(128)}) custom-call(s32[1]{0:T(128)S(4)} %get-tuple-element.176.chosen_ref, f32[1]{0:T(128)S(4)} %get-tuple-element.177.p_ref, f32[2,128,256]{2,1,0:T(8,128)S(1)} %get-tuple-element.178.f_ref, s32[1,128]{1,0:T(1,128)S(1)} %get-tuple-element.179.packed_ref, ...), custom_call_target="tpu_custom_call", output_to_operand_aliasing={{0}: (4, {})} | custom-call | tf_op jit(solution)/shard_map/cond/branch_0_fun/cond/branch_1_fun/expand2/pallas_call | solution.py:635

commit v3 on v2

--- a/solution.py
+++ b/solution.py
@@ -225,6 +225,7 @@
 
 def main_kernel(
     level,
+    match,
     x_hbm,
     local_hbm,
     top_hbm,
@@ -247,6 +248,7 @@
     in_buf,
     back_out,
     back_in,
+    sums_in,
     in_sem,
     send_sem,
     recv_sem,
@@ -288,7 +290,7 @@
     if not shared:
         each_core(NEAR, enter)
         enter((0, 0, 0, 0), 1)
-    for load in loads[:6]:
+    for load in loads[:5]:
         load.wait()
 
     legs = [[placement[t, i] for i in range(7)] for t in range(5)]
@@ -316,6 +318,7 @@
     mid = complex_rows(mid)
     mid = split(mid[:128] if shared else mid)
 
+    loads[5].wait()
     rows = jnp.concatenate(
         [
             jnp.concatenate(
@@ -420,6 +423,23 @@
     own_back = pltpu.make_async_copy(
         block(back_out, place.column, per_back), block(back_in, slot, per_back), own_sem.at[1]
     )
+
+    total_row = back_out.at[pl.ds(per_block, 1)]
+    matches = [lax.div(y, 2) == (0 if match is None else match) for y in place.ys]
+
+    def send_sums(offset, other):
+        pltpu.make_async_remote_copy(
+            src_ref=total_row,
+            dst_ref=block(sums_in, slot, 1),
+            send_sem=send_sem.at[2],
+            recv_sem=recv_sem.at[2],
+            device_id=place.device(offset, other),
+            device_id_type=MESH,
+        ).start()
+
+    def to_both(dy, act):
+        pl.when(matches[dy])(functools.partial(act, send_back))
+        pl.when(jnp.logical_not(matches[dy]))(functools.partial(act, send_sums))
 
     def fold(norm, kept):
         return jnp.where(
@@ -464,24 +484,55 @@
             sums = fold(norm[:, :128] + norm[:, 128:], kept[:, :128] + kept[:, 128:])
             back_out[pl.ds(2, 8, stride=3), :] = jnp.broadcast_to(sums, (8, 128))
             pl.semaphore_wait(ready_sem, 64)
-            each_other(send_back)
-            own_back.start()
-            own_back.wait()
-            wait_for(back_in, 63 * 3, recv_sem.at[1])
+            for offsets in FAR + NEAR:
+                for dy in (2, 1, 3, 0):
+                    group = [o for o in offsets if o[0] == dy]
+                    if group:
+                        to_both(dy, functools.partial(each_core, [group]))
+            to_both(0, lambda act: act((0, 0, 0, 0), 1))
+
+            @pl.when(matches[0])
+            def _():
+                own_back.start()
+                own_back.wait()
+                wait_for(back_in, 63 * 3, recv_sem.at[1])
+
+            @pl.when(jnp.logical_not(matches[0]))
+            def _():
+                own_sums = pltpu.make_async_copy(total_row, block(sums_in, slot, 1), own_sem.at[1])
+                own_sums.start()
+                own_sums.wait()
+                wait_for(sums_in, 63, recv_sem.at[2])
 
         @pl.when(jnp.logical_not(place.owner))
         def _():
-            wait_for(back_in, 64 * 3, recv_sem.at[1])
-
-        finish(
-            back_in[pl.ds(2, 64, stride=3), :],
-            [(0, n * 64, 64, 0, back_in[pl.ds(n, 64, stride=3), :]) for n in range(2)],
-        )
+            pl.when(matches[0])(lambda: wait_for(back_in, 64 * 3, recv_sem.at[1]))
+            pl.when(jnp.logical_not(matches[0]))(lambda: wait_for(sums_in, 64, recv_sem.at[2]))
+
+        @pl.when(matches[0])
+        def _():
+            finish(
+                back_in[pl.ds(2, 64, stride=3), :],
+                [(0, n * 64, 64, 0, back_in[pl.ds(n, 64, stride=3), :]) for n in range(2)],
+            )
+
+        @pl.when(jnp.logical_not(matches[0]))
+        def _():
+            finish(sums_in[...], [])
 
         @pl.when(place.owner)
         def _():
             wait_for(out_buf, 63 * 2, send_sem.at[0])
-            wait_for(x_ref, 127 * 3, send_sem.at[1])
+
+            @pl.when(matches[0])
+            def _():
+                wait_for(x_ref, 63 * 3, send_sem.at[1])
+                wait_for(x_ref, 64, send_sem.at[2])
+
+            @pl.when(jnp.logical_not(matches[0]))
+            def _():
+                wait_for(x_ref, 64 * 3, send_sem.at[1])
+                wait_for(x_ref, 63, send_sem.at[2])
 
         @pl.when(jnp.logical_not(place.owner))
         def _():
@@ -583,7 +634,10 @@
     p_copy.wait()
 
 
-def run_level(level, buffer, x, local_gates, top_gates, placement, damping, branches, outcomes):
+KERNELS = ((0, None), (1, None), (2, None), (3, None), (4, 0), (4, 1))
+
+
+def run_level(level, match, buffer, x, local_gates, top_gates, placement, damping, branches, outcomes):
     shared, parts, groups, _ = layout(level)
     per_block = 2 if shared else parts * groups
     per_back = per_block + 1
@@ -592,7 +646,7 @@
     hbm = pl.BlockSpec(memory_space=pltpu.HBM)
     smem = pl.BlockSpec(memory_space=pltpu.SMEM)
     packed, rows, chosen, probability = pl.pallas_call(
-        functools.partial(main_kernel, level),
+        functools.partial(main_kernel, level, match),
         out_shape=(
             pltpu.VMEM((parts, 128, 128 * groups), F32),
             pltpu.VMEM((1, 128), I32),
@@ -613,14 +667,15 @@
             pltpu.VMEM((128 * per_block, 128), F32),
             pltpu.VMEM((8 * per_back, 128), F32),
             pltpu.VMEM((owners * per_back, 128), F32),
+            pltpu.VMEM((64, 128), F32),
             pltpu.SemaphoreType.DMA((7,)),
-            pltpu.SemaphoreType.DMA((2,)),
-            pltpu.SemaphoreType.DMA((2,)),
+            pltpu.SemaphoreType.DMA((3,)),
+            pltpu.SemaphoreType.DMA((3,)),
             pltpu.SemaphoreType.DMA((2,)),
             pltpu.SemaphoreType.REGULAR,
         ],
         compiler_params=pltpu.CompilerParams(
-            collective_id=level + 1, has_side_effects=True, vmem_limit_bytes=32 * 1024 * 1024
+            collective_id=KERNELS.index((level, match)) + 1, has_side_effects=True, vmem_limit_bytes=32 * 1024 * 1024
         ),
         name=f"window{level}",
     )(
@@ -653,58 +708,60 @@
     )
 
 
-def level_kernel(branches_hbm, *rest):
-    *choice_refs, out_hbm, branches, zeros, sem, sems = rest
-    load = pltpu.make_async_copy(branches_hbm, branches, sem)
-    load.start()
+def level_kernel(branches_hbm, outcomes_hbm, *rest):
+    *choice_refs, out_hbm, branches, outcomes, zeros, in_sem, sems = rest
+    loads = [
+        pltpu.make_async_copy(branches_hbm, branches, in_sem.at[0]),
+        pltpu.make_async_copy(outcomes_hbm, outcomes, in_sem.at[1]),
+    ]
+    for load in loads:
+        load.start()
     zeros[...] = jnp.zeros((256, 128), F32)
     fill_rows(zeros, out_hbm, sems, 0)
-    load.wait()
+    for load in loads:
+        load.wait()
     jumps = branches[0]
     for i in range(1, 7):
         jumps = jumps + branches[i]
-    for limit, choice_ref in enumerate(choice_refs):
+    choice_refs[4][0] = outcomes[0]
+    for limit, choice_ref in enumerate(choice_refs[:4]):
         choice_ref[0] = jnp.where(jumps > limit, 1, 0)
 
 
-def choose_level(branches):
+def choose_level(branches, outcomes):
     return pl.pallas_call(
         level_kernel,
-        out_shape=(pltpu.SMEM((1,), I32),) * 4 + (pltpu.HBM((2048, 128), F32),),
-        in_specs=[pl.BlockSpec(memory_space=pltpu.HBM)],
-        out_specs=(pl.BlockSpec(memory_space=pltpu.SMEM),) * 4
+        out_shape=(pltpu.SMEM((1,), I32),) * 5 + (pltpu.HBM((2048, 128), F32),),
+        in_specs=[pl.BlockSpec(memory_space=pltpu.HBM)] * 2,
+        out_specs=(pl.BlockSpec(memory_space=pltpu.SMEM),) * 5
         + (pl.BlockSpec(memory_space=pltpu.HBM),),
         scratch_shapes=[
             pltpu.SMEM((7,), I32),
+            pltpu.SMEM((4,), I32),
             pltpu.VMEM((256, 128), F32),
-            pltpu.SemaphoreType.DMA,
+            pltpu.SemaphoreType.DMA((2,)),
             pltpu.SemaphoreType.DMA((4,)),
         ],
         name="level",
-    )(branches)
+    )(branches, outcomes)
 
 
 def shards(initial_state, *small):
-    *more, buffer = choose_level(small[4])
-    level = [functools.partial(run_level, n) for n in range(5)]
-
-    def either(choice, otherwise, then):
+    *more, buffer = choose_level(small[4], small[5])
+
+    def kernel(level, match=None):
+        return lambda _, *args: run_level(level, match, *args)
+
+    def choose(choice, otherwise, then):
         return lambda choices, *args: lax.switch(
-            choices[choice][0],
-            [lambda _, *a: otherwise(*a), lambda _, *a: then(*a)],
-            None,
-            *args,
+            choices[choice][0], [otherwise, then], choices, *args
         )
 
-    def two(choice, low, high):
-        return lambda choices, *args: lax.switch(
-            choices[choice][0],
-            [lambda c, *a: low(c, *a), lambda c, *a: high(c, *a)],
-            choices,
-            *args,
-        )
-
-    tree = two(2, two(1, either(0, level[0], level[1]), lambda c, *a: level[2](*a)), either(3, level[3], level[4]))
+    tree = choose(
+        2,
+        choose(1, choose(0, kernel(0), kernel(1)), kernel(2)),
+        choose(3, kernel(3), choose(4, kernel(4, 0), kernel(4, 1))),
+    )
     collapsed, probability = lax.optimization_barrier(
         tree(tuple(more), buffer, initial_state.reshape(2048, 128), *small)
     )

time: 28.4 us -> 23.5 us (0.83)
  Pallas kernels: 26.6 us -> 22.4 us
  loops' own time: 0.77 us -> 0.3 us
    pallas_call x2, Pallas kernels: 25.8 us -> 21.5 us  [the longest x1 20.7 us: run_level(): pl.pallas_call(functools.partial(main_kernel, level, match), out_shape=(p...]
    another operation x2 -> x3, loops' own time: 0.77 us -> 0.3 us  [choose(): lax.switch(choices[choice][0], [otherwise, then], choices, *args)]
where the time goes in v3:
time: 23.5 us
  Pallas kernels  22.4 us (95%)
  between operations  0.82 us (3%)
  loops' own time  0.3 us (1%)
    pallas_call x1, Pallas kernels, run_level(): pl.pallas_call(functools.partial(main_kernel, level, match), out_shape=(p...  20.7 us
    pallas_call x1, Pallas kernels, choose_level(): pl.pallas_call(level_kernel, out_shape=(pltpu.SMEM((1,), I32),) * 5 + (pl...  0.88 us
    pallas_call x1, Pallas kernels, run_level(): pl.pallas_call(functools.partial(expand_kernel, level), out_shape=(pltpu....  0.86 us

profile of v3, /device:TPU:1, one launch (start us, length us, event | category | flops | bytes accessed | tf_op | source)
XLA Modules:
  0.0 23.5 jit_solution(16661921922098531170)
XLA Ops:
  0.6 0.9 %level.1 = (s32[1]{0:T(128)S(4)}, s32[1]{0:T(128)S(4)}, s32[1]{0:T(128)S(4)}, s32[1]{0:T(128)S(4)}, s32[1]{0:T(128)S(4)}, /*index=5*/f32[2048,128]{1,0:T(8,128)}) custom-call(s32[7]{0:T(128)} %branches_hbm.1, s32[4]{0:T(128)} %outcomes_hbm.1), custom_call_target="tpu_custom_call" | custom-call | tf_op jit(solution)/shard_map/level/pallas_call | solution.py:732
  1.5 21.8 %conditional.5 = ((f32[2048,128]{1,0:T(8,128)}, f32[1]{0:T(128)})) conditional(s32[]{:T(128)} %bitcast.4, (s32[1]{0:T(128)S(4)}, s32[1]{0:T(128)S(4)}, f32[2048,128]{1,0:T(8,128)}, f32[3,2,128,128]{3,2,1,0:T(8,128)}, f32[2,2,128,128]{3,2,1,0:T(8,128)}, /*index=5*/s32[5,7]{1,0:T(8,128)}, f32[7]{0:T(128)}, s32[7]{0:T(128)}, s32[4]{0:T(128)}, ...), branch_computations={%region_0.0_spmd, %region_5.0_spmd} | conditional | flops 2 | bytes 240 | solution.py:756
  1.8 21.6 %conditional.3 = ((f32[2048,128]{1,0:T(8,128)}, f32[1]{0:T(128)})) conditional(s32[]{:T(128)} %bitcast.3, (f32[2048,128]{1,0:T(8,128)}, f32[3,2,128,128]{3,2,1,0:T(8,128)}, f32[2,2,128,128]{3,2,1,0:T(8,128)}, s32[5,7]{1,0:T(8,128)}, f32[7]{0:T(128)}, /*index=5*/s32[7]{0:T(128)}, s32[4]{0:T(128)}, f32[2048,128]{1,0:T(8,128)}) %tuple.32, ...), branch_computations={%region_6.0_spmd, %region_7.0_spmd} | conditional | flops 1 | bytes 88 | solution.py:756
  1.8 21.6 %conditional.2 = ((f32[2048,128]{1,0:T(8,128)}, f32[1]{0:T(128)})) conditional(s32[]{:T(128)} %bitcast.2, (f32[2048,128]{1,0:T(8,128)}, f32[3,2,128,128]{3,2,1,0:T(8,128)}, f32[2,2,128,128]{3,2,1,0:T(8,128)}, s32[5,7]{1,0:T(8,128)}, f32[7]{0:T(128)}, /*index=5*/s32[7]{0:T(128)}, s32[4]{0:T(128)}, f32[2048,128]{1,0:T(8,128)}) %tuple.30, ...), branch_computations={%region_8.0_spmd, %region_9.0_spmd} | conditional | bytes 8 | solution.py:756
  1.8 20.7 %window4.2 = (f32[1,128,128]{2,1,0:T(8,128)S(1)}, s32[1,128]{1,0:T(1,128)S(1)}, s32[1]{0:T(128)S(4)}, f32[1]{0:T(128)S(4)}) custom-call(f32[2048,128]{1,0:T(8,128)} %get-tuple-element.239.x_hbm, f32[3,2,128,128]{3,2,1,0:T(8,128)} %get-tuple-element.240.local_hbm, f32[2,2,128,128]{3,2,1,0:T(8,128)} %get-tuple-element.241.top_hbm, ...), custom_call_target="tpu_custom_call" | custom-call | tf_op jit(solution)/shard_map/cond/branch_1_fun/cond/branch_1_fun/cond/branch_0_fun/window4/pallas_call | solution.py:648
  22.5 0.9 %expand4.2 = (f32[2048,128]{1,0:T(8,128)}, f32[1]{0:T(128)}) custom-call(s32[1]{0:T(128)S(4)} %get-tuple-element.246.chosen_ref, f32[1]{0:T(128)S(4)} %get-tuple-element.247.p_ref, f32[1,128,128]{2,1,0:T(8,128)S(1)} %get-tuple-element.248.f_ref, s32[1,128]{1,0:T(1,128)S(1)} %get-tuple-element.249.packed_ref, ...), custom_call_target="tpu_custom_call", output_to_operand_aliasing={{0}: (4, {})} | custom-call | tf_op jit(solution)/shard_map/cond/branch_1_fun/cond/branch_1_fun/cond/branch_0_fun/expand4/pallas_call | solution.py:690
